TPU v7x, 32 devices: a whole 2x2x4 slice. The times are simulated.
32 devices in a mesh: seq: 2 (over x), sect: 4 (over y, core), mp: 4 (over z).
Axes of the slice: x: 2, y: 2, z: 4, core: 2. Of those that a mesh axis runs over, the one named last changes fastest.
Arguments:
- enc_query: bfloat16 [4, 256, 2048], P('sect', 'seq', 'mp'), may hold values from -15 to 15
- enc_keys: bfloat16 [4, 256, 2048], P('sect', 'seq', 'mp'), may hold values from -6 to 6
- enc_values: bfloat16 [4, 256, 2048], P('sect', 'seq', 'mp'), may hold values from -6 to 6
- enc_lengths: int32 [4], replicated, may hold values from 192 to 256, as said below
- cross_keys: bfloat16 [4, 256, 2048], P('sect', 'seq', 'mp'), may hold values from -6 to 6
- cross_values: bfloat16 [4, 256, 2048], P('sect', 'seq', 'mp'), may hold values from -6 to 6
- cross_query: bfloat16 [128, 4, 512], P('seq', 'mp', 'sect'), may hold values from -15 to 15
- dec_query: bfloat16 [128, 4, 512], P('seq', 'mp', 'sect'), may hold values from -15 to 15
- dec_keys: bfloat16 [128, 4, 512], P('seq', 'mp', 'sect'), may hold values from -6 to 6
- dec_values: bfloat16 [128, 4, 512], P('seq', 'mp', 'sect'), may hold values from -6 to 6
- cross_out_weight: bfloat16 [4, 512, 4096], P('mp', 'sect'), may hold values from -0.125 to 0.125
- dec_hidden: bfloat16 [128, 4096], P('seq', ('sect', 'mp')), may hold values from -6 to 6
Outputs:
- enc_context: bfloat16 [4, 256, 2048], P('sect', 'seq', 'mp')
- self_context: bfloat16 [128, 4, 512], P('seq', 'mp', 'sect')
- decoded: bfloat16 [128, 4096], P('seq', ('sect', 'mp'))
Inputs may be any that keep to these rules, and one draw needn't show every extreme that they name: `enc_lengths`: at least one micro-batch has all 256 positions valid.
All inputs are finite; a program needn't handle non-finite values.
Results may differ from a plain program's by a relative error of at most 0.012.
Values may be sent and summed in bfloat16 or wider, within the bound.
A program may use at most 128 MiB of HBM per device.

v0:
```python
import jax
import jax.numpy as jnp
from jax import lax
from jax.sharding import PartitionSpec as P

HEAD_DIM = 64


def broadcast(array, axis, root):
    mine = lax.axis_index(axis) == root
    return lax.psum(jnp.where(mine, array, jnp.zeros_like(array)), axis)


def start_running(head_count, rows):
    return (
        jnp.zeros((head_count, rows, HEAD_DIM), jnp.float32),
        jnp.full((head_count, rows), -1e30, jnp.float32),
        jnp.zeros((head_count, rows), jnp.float32),
    )


def accumulate(running, queries, key_rows, values, allowed):
    summed, highest, weight_sum = running
    scores = jnp.einsum("hqe,khe->hqk", queries, key_rows, preferred_element_type=jnp.float32)
    new_high = jnp.maximum(highest, jnp.max(jnp.where(allowed, scores, -1e30), axis=2))
    weights = jnp.where(allowed, jnp.exp(scores - new_high[:, :, None]), 0.0)
    rounded = weights.astype(jnp.bfloat16)
    total = jnp.sum(weights, axis=2)
    update = jnp.einsum("hqk,khe->hqe", rounded, values, preferred_element_type=jnp.float32)
    return (update, new_high, total)


def finish(running):
    summed, highest, weight_sum = running
    context = summed / weight_sum[:, :, None]
    return context.transpose(1, 0, 2).reshape(context.shape[1], -1).astype(jnp.bfloat16)


def head_major(block, rows):
    scaled = block * HEAD_DIM ** (-0.5)
    return scaled.reshape(rows, -1, HEAD_DIM).transpose(1, 0, 2)


def per_device(
    enc_query,
    enc_keys,
    enc_values,
    enc_lengths,
    cross_keys,
    cross_values,
    cross_query,
    dec_query,
    dec_keys,
    dec_values,
    cross_out_weight,
    dec_hidden,
):
    enc_rows = enc_query.shape[1]
    dec_rows = cross_query.shape[0]
    narrow = cross_query.shape[2]
    section = lax.axis_index("sect")
    own_limit = lax.dynamic_index_in_dim(enc_lengths, section, 0, False)
    root_limit = enc_lengths[0]
    enc_heads = head_major(enc_query[0], enc_rows)
    cross_heads = head_major(cross_query[:, 0, :], dec_rows)
    root_pair = (broadcast(cross_keys, "sect", 0), broadcast(cross_values, "sect", 0))
    offset = section * narrow
    cross_key_rows = lax.dynamic_slice_in_dim(root_pair[0], offset, narrow, 2)
    cross_value_rows = lax.dynamic_slice_in_dim(root_pair[1], offset, narrow, 2)
    enc_init = start_running(enc_heads.shape[0], enc_rows)
    cross_init = start_running(cross_heads.shape[0], dec_rows)
    pieces = (
        lax.all_gather(enc_keys, "seq", axis=1, tiled=True),
        lax.all_gather(enc_values, "seq", axis=1, tiled=True),
    )
    key_rows = pieces[0]
    length = key_rows.shape[1]
    allowed = (jnp.arange(length, dtype=jnp.int32) < own_limit)[None, None, :]
    enc_running = accumulate(
        enc_init,
        enc_heads,
        key_rows[0].reshape(length, -1, HEAD_DIM),
        pieces[1][0].reshape(length, -1, HEAD_DIM),
        allowed,
    )
    pieces = (
        lax.all_gather(cross_key_rows, "seq", axis=1, tiled=True),
        lax.all_gather(cross_value_rows, "seq", axis=1, tiled=True),
    )
    key_rows = pieces[0]
    length = key_rows.shape[1]
    allowed = (jnp.arange(length, dtype=jnp.int32) < root_limit)[None, None, :]
    cross_running = accumulate(
        cross_init,
        cross_heads,
        key_rows[0].reshape(length, -1, HEAD_DIM),
        pieces[1][0].reshape(length, -1, HEAD_DIM),
        allowed,
    )
    enc_context = finish(enc_running).reshape(1, enc_rows, -1)
    dec_heads = head_major(dec_query[:, 0, :], dec_rows)
    query_positions = lax.axis_index("seq") * dec_rows + jnp.arange(dec_rows, dtype=jnp.int32)
    pieces = (
        lax.all_gather(dec_keys, "seq", axis=0, tiled=True),
        lax.all_gather(dec_values, "seq", axis=0, tiled=True),
    )
    length = pieces[0].shape[0]
    key_positions = jnp.arange(length, dtype=jnp.int32)
    allowed = (key_positions[None, :] <= query_positions[:, None])[None, :, :]
    self_running = accumulate(
        start_running(dec_heads.shape[0], dec_rows),
        dec_heads,
        pieces[0].reshape(length, -1, HEAD_DIM),
        pieces[1].reshape(length, -1, HEAD_DIM),
        allowed,
    )
    self_context = finish(self_running).reshape(dec_rows, 1, narrow)
    cross_context = finish(cross_running)
    weight = cross_out_weight[0]
    projected = (
        lax.psum_scatter(
            lax.dot_general(
                weight, cross_context, (((0,), (1,)), ((), ())), preferred_element_type=jnp.float32
            ).astype(jnp.bfloat16),
            ("sect", "mp"),
            scatter_dimension=0,
            tiled=True,
        )
        .astype(jnp.float32)
        .T
    )
    decoded = (dec_hidden.astype(jnp.float32) + projected).astype(jnp.bfloat16)
    return (enc_context, self_context, decoded)


def solution(mesh):
    in_specs = (
        P("sect", "seq", "mp"),
        P("sect", "seq", "mp"),
        P("sect", "seq", "mp"),
        P(),
        P("sect", "seq", "mp"),
        P("sect", "seq", "mp"),
        P("seq", "mp", "sect"),
        P("seq", "mp", "sect"),
        P("seq", "mp", "sect"),
        P("seq", "mp", "sect"),
        P("mp", "sect", None),
        P("seq", ("sect", "mp")),
    )
    out_specs = (P("sect", "seq", "mp"), P("seq", "mp", "sect"), P("seq", ("sect", "mp")))
    return jax.shard_map(
        per_device, mesh=mesh, in_specs=in_specs, out_specs=out_specs, check_vma=False
    )
```

profile of v0, /device:TPU:0, one launch (start us, length us, event | category | flops | bytes accessed | tf_op | source)
XLA Modules:
  0.0 122.3 jit_solution(17426027138814709747)
XLA Ops:
  7.2 1.8 %broadcast_select_fusion = (bf16[1,128,512]{2,1,0:T(8,128)(2,1)}, bf16[1,128,512]{2,1,0:T(8,128)(2,1)}) fusion(bf16[1,128,512]{2,1,0:T(8,128)(2,1)} %param.17, pred[]{:T(512)S(6)} %eq.4, bf16[1,128,512]{2,1,0:T(8,128)(2,1)} %param.16), kind=kLoop, calls=%fused_computation.21 | loop fusion | flops 131072 | bytes 524289 | tf_op jit(solution)/shard_map/jit(_where)/select_n | solution.py:11
  9.1 0.6 copy-done.7
  9.7 0.6 copy-done.9
  10.4 0.6 fusion.36
  11.0 0.6 iota_compare_fusion.2
  11.6 6.5 %all_gather.18 = bf16[1,256,512]{2,1,0:T(8,128)(2,1)S(1)} all-gather(bf16[1,128,512]{2,1,0:T(8,128)(2,1)S(1)} %copy-done.1), channel_id=1, replica_groups=mesh['seq'=2,'sect'=4,'mp'=4] {'seq'}, dimensions={1}, use_global_device_ids=true | all-gather | bytes 393216 | tf_op jit(solution)/shard_map/all_gather | solution.py:73
  18.3 0.8 copy-done.3
  19.7 0.5 copy-done.2
  20.1 5.6 %all_gather.19 = bf16[1,256,512]{2,1,0:T(8,128)(2,1)S(1)} all-gather(bf16[1,128,512]{2,1,0:T(8,128)(2,1)S(1)} %copy-done.2), channel_id=1, replica_groups=mesh['seq'=2,'sect'=4,'mp'=4] {'seq'}, dimensions={1}, use_global_device_ids=true | all-gather | bytes 393216 | tf_op jit(solution)/shard_map/all_gather | solution.py:74
  25.9 0.6 copy-done.8
  27.4 0.8 copy.36
  28.2 4.5 %all_gather.20 = bf16[128,1,128]{2,0,1:T(8,128)(2,1)S(1)} all-gather(bf16[64,1,128]{2,0,1:T(8,128)(2,1)S(1)} %copy-done.5), channel_id=1, replica_groups=mesh['seq'=2,'sect'=4,'mp'=4] {'seq'}, dimensions={0}, use_global_device_ids=true | all-gather | bytes 49152 | tf_op jit(solution)/shard_map/all_gather | solution.py:104
  32.9 0.6 copy-done.6
  33.5 4.4 %all_gather.21 = bf16[128,1,128]{2,0,1:T(8,128)(2,1)S(1)} all-gather(bf16[64,1,128]{2,0,1:T(8,128)(2,1)S(1)} %copy-done.6), channel_id=1, replica_groups=mesh['seq'=2,'sect'=4,'mp'=4] {'seq'}, dimensions={0}, use_global_device_ids=true | all-gather | bytes 49152 | tf_op jit(solution)/shard_map/all_gather | solution.py:105
  38.0 0.7 iota_compare_fusion.1
  38.7 6.5 %all-reduce.3.cloned.1.call-done = (bf16[1,128,512]{2,1,0:T(8,128)(2,1)}, bf16[1,128,512]{2,1,0:T(8,128)(2,1)}) async-done(((bf16[1,128,512]{2,1,0:T(8,128)(2,1)}, bf16[1,128,512]{2,1,0:T(8,128)(2,1)}), (bf16[1,128,512]{2,1,0:T(8,128)(2,1)}, bf16[1,128,512]{2,1,0:T(8,128)(2,1)})) %all-reduce.3.cloned.1.call-update) | async-done | bytes 262160 | tf_op jit(solution)/shard_map/psum | solution.py:11
  45.3 0.8 constant_dynamic-slice_fusion.1
  46.0 4.6 %all_gather.22 = bf16[1,256,128]{2,1,0:T(8,128)(2,1)S(1)} all-gather(bf16[1,128,128]{2,1,0:T(8,128)(2,1)S(1)} %constant_dynamic-slice_fusion.1), channel_id=1, replica_groups=mesh['seq'=2,'sect'=4,'mp'=4] {'seq'}, dimensions={1}, use_global_device_ids=true | all-gather | bytes 98304 | tf_op jit(solution)/shard_map/all_gather | solution.py:87
  50.9 0.8 constant_dynamic-slice_fusion
  51.7 4.6 %all_gather.23 = bf16[1,256,128]{2,1,0:T(8,128)(2,1)S(1)} all-gather(bf16[1,128,128]{2,1,0:T(8,128)(2,1)S(1)} %constant_dynamic-slice_fusion), channel_id=1, replica_groups=mesh['seq'=2,'sect'=4,'mp'=4] {'seq'}, dimensions={1}, use_global_device_ids=true | all-gather | bytes 98304 | tf_op jit(solution)/shard_map/all_gather | solution.py:88
  57.0 1.1 fusion
  58.7 0.7 convert_element_type.59
  59.4 54.6 %reduce-scatter.2.cloned.1.call-done = bf16[256,64]{0,1:T(8,128)(2,1)} async-done(((bf16[4096,64]{0,1:T(8,128)(2,1)}), bf16[256,64]{0,1:T(8,128)(2,1)}) %reduce-scatter.2.cloned.1.call-update) | async-done | bytes 32784 | tf_op jit(solution)/shard_map/reduce_scatter | solution.py:121
  114.1 1.4 %fusion.17 = bf16[64,256]{1,0:T(8,128)(2,1)} fusion(bf16[256,64]{0,1:T(8,128)(2,1)} %reduce-scatter.2.cloned.1.call-done, bf16[64,256]{1,0:T(8,128)(2,1)S(1)} %copy-done.4), kind=kLoop, calls=%fused_computation.26 | loop fusion | flops 65536 | bytes 98304 | tf_op jit(solution)/shard_map/convert_element_type | solution.py:132
  (47 shorter events, 3.8 us)
Async XLA Ops:
  7.2 49.8 %copy-start = (bf16[1,128,4096]{2,1,0:T(8,128)(2,1)S(1)}, bf16[1,128,4096]{2,1,0:T(8,128)(2,1)}, u32[]{:S(2)}) copy-start(bf16[1,128,4096]{2,1,0:T(8,128)(2,1)} %param.22) | copy-start | bytes 3145732
  7.2 38.1 %all-reduce.3.cloned.1.call-start = ((), (), s32[]{:S(2)}) async-start(), calls=%async_computation.2 | async-start | bytes 524288 | tf_op jit(solution)/shard_map/psum | solution.py:11
  9.0 0.7 copy-start.7
  9.0 2.6 %copy-start.1 = (bf16[1,128,512]{2,1,0:T(8,128)(2,1)S(1)}, bf16[1,128,512]{2,1,0:T(8,128)(2,1)}, u32[]{:S(2)}) copy-start(bf16[1,128,512]{2,1,0:T(8,128)(2,1)} %param.13) | copy-start | bytes 393220
  9.0 105.0 %reduce-scatter.2.cloned.1.call-start = ((), (), s32[]{:S(2)}) async-start(), calls=%async_computation.1 | async-start | bytes 557056 | tf_op jit(solution)/shard_map/reduce_scatter | solution.py:121
  9.7 0.7 copy-start.9
  18.2 0.9 copy-start.3
  19.2 0.9 copy-start.2
  25.8 0.7 copy-start.8
  27.4 0.8 copy-start.5
  32.8 0.7 copy-start.6
  58.7 55.3 %copy-start.4 = (bf16[64,256]{1,0:T(8,128)(2,1)S(1)}, bf16[64,256]{1,0:T(8,128)(2,1)}, u32[]{:S(2)}) copy-start(bf16[64,256]{1,0:T(8,128)(2,1)} %param.23) | copy-start | bytes 98308
Sparse Core Ops, SparseCore 0:
  10.4 34.7 all-reduce.2
  58.2 55.8 reduce-scatter.1
where the time goes:
time: 123 us; the launch traced here: 122 us
  waiting for transfers between devices  61.2 us (50%)
  blocking collectives  30.2 us (25%)
  between operations  14.3 us (12%)
  local copies, waits for them, and re-layouts  8.46 us (7%)
  other arithmetic  5.31 us (4%)
  matrix products  2.77 us (2%)
    reduce_scatter x1, waiting for transfers between devices, per_device(): lax.psum_scatter(lax.dot_general(weight, cross_context, (((0,), (1,)), ((...  54.6 us
    psum x1, waiting for transfers between devices, broadcast(): return lax.psum(jnp.where(mine, array, jnp.zeros_like(array)), axis)  6.54 us
    all_gather x1, blocking collectives, per_device(): lax.all_gather(enc_keys, 'seq', axis=1, tiled=True)  6.54 us
    all_gather x1, blocking collectives, per_device(): lax.all_gather(enc_values, 'seq', axis=1, tiled=True)  5.63 us
    unnamed x22, local copies, waits for them, and re-layouts  4.64 us
    all_gather x1, blocking collectives, per_device(): lax.all_gather(cross_key_rows, 'seq', axis=1, tiled=True)  4.58 us
    all_gather x1, blocking collectives, per_device(): lax.all_gather(cross_value_rows, 'seq', axis=1, tiled=True)  4.58 us
    all_gather x1, blocking collectives, per_device(): lax.all_gather(dec_keys, 'seq', axis=0, tiled=True)  4.49 us
  transfers between devices with their start and end apart: 2, of which 2 were waited for; matrix products, arithmetic and copies ran while one was open for 5% of the time, Pallas kernels for 0%

commit v1 on v0

v1 whole, which is shorter than its diff:
```python
import functools
import math

import jax
import jax.numpy as jnp
from jax import lax
from jax.experimental import pallas as pl
from jax.experimental.pallas import tpu as pltpu
from jax.sharding import PartitionSpec as P

HEAD_DIM = 64
PAIR = 2 * HEAD_DIM
FACTOR = HEAD_DIM ** (-0.5) * math.log2(math.e)
LOW = -1e30
SECTIONS = 4
F32 = jnp.float32
BF16 = jnp.bfloat16


def each(low, high, body):
    if high - low <= 4:
        for step in range(low, high):
            body(step)
    else:
        lax.fori_loop(low, high, lambda step, carry: (body(step), carry)[1], 0)


def stack_heads(queries):
    lane = lax.broadcasted_iota(jnp.int32, queries.shape, 1)
    wide = queries.astype(F32)
    first = jnp.where(lane < HEAD_DIM, wide, 0.0).astype(BF16)
    second = jnp.where(lane < HEAD_DIM, 0.0, wide).astype(BF16)
    return jnp.concatenate([first, second], axis=0)


def attend(stacked, keys, values, bias):
    scores = lax.dot_general(stacked, keys, (((1,), (1,)), ((), ())), preferred_element_type=F32)
    scores = scores * FACTOR + bias
    high = jnp.max(scores, axis=1, keepdims=True)
    weights = jnp.exp2(scores - high).astype(BF16)
    wide = jnp.concatenate([values, jnp.ones_like(values)], axis=1)
    return jnp.dot(weights, wide, preferred_element_type=F32), high


def merge_heads(summed):
    context = summed[:, :PAIR] / summed[:, PAIR:]
    rows = context.shape[0] // 2
    lane = lax.broadcasted_iota(jnp.int32, (rows, PAIR), 1)
    return jnp.where(lane < HEAD_DIM, context[:rows], context[rows:]).astype(BF16)


def kernel(
    n, mps,
    eq, ek, ev, lengths, ck, cv, cq, dq, dk, dv, weight, hidden,
    enc_out, self_out, dec_out,
    q_v, ekb, evb, xkb, xvb, cq_v, dq_v, dkb, dvb, w_v, hid_v,
    acc, highs, ctx, ctx_in, y_out, y_in, own, z_out, z_in,
    load_sem, enc_send, enc_recv, x_send, x_recv, dec_send, dec_recv,
    w_send, w_recv, w_load, ctx_send, ctx_recv, y_send, y_recv, z_send, z_recv,
):
    seq, sect, mp = lax.axis_index("seq"), lax.axis_index("sect"), lax.axis_index("mp")
    enc_rows, enc_width = q_v.shape
    dec_rows = cq_v.shape[0]
    block = hid_v.shape[1]
    span = mps * block
    near = sect + 1 - 2 * lax.rem(sect, 2)
    far = lax.rem(sect + 2, SECTIONS)
    core = lax.rem(sect, 2)
    level = sect // 2
    MESH = pl.DeviceIdType.MESH

    def remote(source, target, send, recv, device):
        return pltpu.make_async_remote_copy(
            src_ref=source, dst_ref=target, send_sem=send, recv_sem=recv,
            device_id=device, device_id_type=MESH,
        )

    def peer(step):
        return lax.rem(seq + step, n)

    def landed(ref, sem):
        pltpu.make_async_copy(ref, ref, sem).wait()

    loads = [
        pltpu.make_async_copy(eq, q_v, load_sem.at[0]),
        pltpu.make_async_copy(cq, cq_v, load_sem.at[1]),
        pltpu.make_async_copy(dq, dq_v, load_sem.at[2]),
        pltpu.make_async_copy(hidden, hid_v, load_sem.at[3]),
        pltpu.make_async_copy(ek, ekb.at[seq], enc_recv.at[0, seq]),
        pltpu.make_async_copy(ev, evb.at[seq], enc_recv.at[1, seq]),
        pltpu.make_async_copy(dk, dkb.at[seq], dec_recv.at[0, seq]),
        pltpu.make_async_copy(dv, dvb.at[seq], dec_recv.at[1, seq]),
    ]
    for load in loads:
        load.start()

    def columns(half, side):
        return pl.ds(pl.multiple_of((2 * half + side) * span, span), span)

    depth = weight.shape[0]
    w_loads = [
        pltpu.make_async_copy(
            weight.at[:, columns(half, core)], w_v.at[half, pl.ds(0, depth)], w_load.at[half]
        )
        for half in range(2)
    ]
    for load in w_loads:
        load.start()

    def first_columns(source):
        return source.at[:, pl.ds(0, PAIR)]

    @pl.when(sect == 0)
    def _():
        pltpu.make_async_copy(first_columns(ck), xkb.at[seq], x_recv.at[0, seq]).start()
        pltpu.make_async_copy(first_columns(cv), xvb.at[seq], x_recv.at[1, seq]).start()

    barrier = pltpu.get_barrier_semaphore()

    def greet(seq_step, sect_step):
        pl.semaphore_signal(
            barrier, inc=1,
            device_id={"seq": peer(seq_step), "sect": lax.rem(sect + sect_step, SECTIONS)},
            device_id_type=MESH,
        )

    for sect_step in range(SECTIONS):
        each(1 if sect_step == 0 else 0, n, lambda step: greet(step, sect_step))
    for step in range(1, mps):
        pl.semaphore_signal(
            barrier, inc=1, device_id={"mp": lax.rem(mp + step, mps)}, device_id_type=MESH
        )
    pl.semaphore_wait(barrier, n * SECTIONS - 1 + mps - 1)

    def cross_copies(step, section):
        device = {"seq": peer(step), "sect": section}
        lanes = pl.ds(section * PAIR, PAIR)
        return [
            remote(source.at[:, lanes], target.at[seq], x_send.at[which, section, step],
                   x_recv.at[which, seq], device)
            for which, source, target in ((0, ck, xkb), (1, cv, xvb))
        ]

    def start_cross(step, section):
        for copy in cross_copies(step, section):
            copy.start()

    def end_cross(step, section):
        for copy in cross_copies(step, section):
            copy.wait_send()

    def all_cross(action):
        for section in (2, 3, 1, 0):
            each(1 if section == 0 else 0, n, lambda step: action(step, section))

    @pl.when(sect == 0)
    def _():
        all_cross(start_cross)

    def seq_copies(step):
        device = {"seq": peer(step)}
        dec = [
            remote(source, target.at[seq], dec_send.at[which, step], dec_recv.at[which, seq], device)
            for which, source, target in ((0, dk, dkb), (1, dv, dvb))
        ]
        enc = [
            remote(source, target.at[seq], enc_send.at[which, step], enc_recv.at[which, seq], device)
            for which, source, target in ((0, ek, ekb), (1, ev, evb))
        ]
        return dec + enc

    def start_seq(step):
        for copy in seq_copies(step):
            copy.start()

    def end_seq(step):
        for copy in seq_copies(step):
            copy.wait_send()

    each(1, n, start_seq)
    w_copies = [
        remote(weight.at[:, columns(half, 1 - core)], w_v.at[half, pl.ds(depth, depth)],
               w_send.at[half], w_recv.at[half], {"sect": near})
        for half in range(2)
    ]
    for copy in w_copies:
        copy.start()

    enc_limit = lengths[sect]
    pairs = enc_width // PAIR

    def enc_chunk(source, first):
        landed(ekb.at[source], enc_recv.at[0, source])
        landed(evb.at[source], enc_recv.at[1, source])
        position = source * enc_rows + lax.broadcasted_iota(jnp.int32, (1, enc_rows), 1)
        bias = jnp.where(position < enc_limit, 0.0, LOW)
        for pair in range(pairs):
            lanes = pl.ds(pair * PAIR, PAIR)
            summed, high = attend(
                stack_heads(q_v[:, lanes]), ekb[source, :, lanes], evb[source, :, lanes], bias
            )
            if first:
                acc[pair] = summed
                highs[pair] = jnp.broadcast_to(high, highs.shape[1:])
            else:
                before = highs[pair][:, :1]
                top = jnp.maximum(before, high)
                acc[pair] = acc[pair] * jnp.exp2(before - top) + summed * jnp.exp2(high - top)
                highs[pair] = jnp.broadcast_to(top, highs.shape[1:])

    loads[0].wait()
    enc_chunk(seq, True)

    loads[1].wait()

    def cross_landed(source):
        landed(xkb.at[source], x_recv.at[0, source])
        landed(xvb.at[source], x_recv.at[1, source])

    each(0, n, cross_landed)
    length = n * enc_rows
    position = lax.broadcasted_iota(jnp.int32, (1, length), 1)
    bias = jnp.where(position < lengths[0], 0.0, LOW)
    summed, _ = attend(
        stack_heads(cq_v[...]), xkb[...].reshape(length, PAIR), xvb[...].reshape(length, PAIR), bias
    )
    ctx[...] = merge_heads(summed)
    ctx_copy = remote(ctx, ctx_in, ctx_send, ctx_recv, {"sect": near})
    ctx_copy.start()

    loads[2].wait()

    def dec_landed(source):
        landed(dkb.at[source], dec_recv.at[0, source])
        landed(dvb.at[source], dec_recv.at[1, source])

    each(0, n, dec_landed)
    length = n * dec_rows
    row = lax.broadcasted_iota(jnp.int32, (2 * dec_rows, length), 0)
    row = jnp.where(row >= dec_rows, row - dec_rows, row) + seq * dec_rows
    position = lax.broadcasted_iota(jnp.int32, (2 * dec_rows, length), 1)
    bias = jnp.where(position <= row, 0.0, LOW)
    summed, _ = attend(
        stack_heads(dq_v[...]), dkb[...].reshape(length, PAIR), dvb[...].reshape(length, PAIR), bias
    )
    self_out[...] = merge_heads(summed)

    for load in w_loads:
        load.wait()
    for copy in w_copies:
        copy.wait_recv()
    ctx_copy.wait_recv()
    both = jnp.concatenate([ctx[...], ctx_in[...]], axis=1)
    order = list(range(1, mps)) + [0]

    def project(half, step):
        owner = lax.rem(mp + step, mps)
        lanes = pl.ds(pl.multiple_of(owner * block, block), block)
        return jnp.dot(both, w_v[half, :, lanes], preferred_element_type=F32)

    y_copies = {}
    for step in order:
        y_out[step] = project(1 - level, step).astype(BF16)
        y_copies[step] = remote(
            y_out.at[step], y_in.at[step], y_send.at[step], y_recv.at[step], {"sect": far}
        )
        y_copies[step].start()
    for step in order:
        own[step] = project(level, step)

    each(1, n, lambda step: enc_chunk(peer(step), False))
    for pair in range(pairs):
        enc_out[:, pair * PAIR:(pair + 1) * PAIR] = merge_heads(acc[pair])

    z_copies = {}
    for step in range(1, mps):
        y_copies[step].wait_recv()
        z_out[step] = (own[step] + y_in[step].astype(F32)).astype(BF16)
        z_copies[step] = remote(
            z_out.at[step], z_in.at[step], z_send.at[step], z_recv.at[step],
            {"mp": lax.rem(mp + step, mps)},
        )
        z_copies[step].start()
    loads[3].wait()
    y_copies[0].wait_recv()
    total = own[0] + y_in[0].astype(F32)
    for step in range(1, mps):
        z_copies[step].wait_recv()
        total = total + z_in[step].astype(F32)
    dec_out[...] = (hid_v[...].astype(F32) + total).astype(BF16)

    @pl.when(sect == 0)
    def _():
        all_cross(end_cross)

    each(1, n, end_seq)
    for copy in w_copies + [ctx_copy] + list(y_copies.values()) + list(z_copies.values()):
        copy.wait_send()


def per_device(
    n, mps, enc_query, enc_keys, enc_values, enc_lengths, cross_keys, cross_values,
    cross_query, dec_query, dec_keys, dec_values, cross_out_weight, dec_hidden,
):
    enc_rows, enc_width = enc_query.shape[1:]
    dec_rows, _, narrow = cross_query.shape
    depth, model = cross_out_weight.shape[1:]
    block = dec_hidden.shape[1]
    span = model // SECTIONS
    pairs = enc_width // PAIR
    vmem, dma = pltpu.VMEM, pltpu.SemaphoreType.DMA
    any_space = pl.BlockSpec(memory_space=pl.ANY)
    in_vmem = pl.BlockSpec(memory_space=pltpu.VMEM)
    enc_out, self_out, decoded = pl.pallas_call(
        functools.partial(kernel, n, mps),
        out_shape=(
            jax.ShapeDtypeStruct((enc_rows, enc_width), BF16),
            jax.ShapeDtypeStruct((dec_rows, narrow), BF16),
            jax.ShapeDtypeStruct((dec_rows, block), BF16),
        ),
        in_specs=[any_space] * 3
        + [pl.BlockSpec(memory_space=pltpu.SMEM)]
        + [any_space] * 8,
        out_specs=(in_vmem,) * 3,
        scratch_shapes=[
            vmem((enc_rows, enc_width), BF16),
            vmem((n, enc_rows, enc_width), BF16),
            vmem((n, enc_rows, enc_width), BF16),
            vmem((n, enc_rows, narrow), BF16),
            vmem((n, enc_rows, narrow), BF16),
            vmem((dec_rows, narrow), BF16),
            vmem((dec_rows, narrow), BF16),
            vmem((n, dec_rows, narrow), BF16),
            vmem((n, dec_rows, narrow), BF16),
            vmem((2, 2 * depth, span), BF16),
            vmem((dec_rows, block), BF16),
            vmem((pairs, 2 * enc_rows, 2 * PAIR), F32),
            vmem((pairs, 2 * enc_rows, PAIR), F32),
            vmem((dec_rows, narrow), BF16),
            vmem((dec_rows, narrow), BF16),
            vmem((mps, dec_rows, block), BF16),
            vmem((mps, dec_rows, block), BF16),
            vmem((mps, dec_rows, block), F32),
            vmem((mps, dec_rows, block), BF16),
            vmem((mps, dec_rows, block), BF16),
            dma((4,)),
            dma((2, n)), dma((2, n)),
            dma((2, SECTIONS, n)), dma((2, n)),
            dma((2, n)), dma((2, n)),
            dma((2,)), dma((2,)), dma((2,)),
            dma, dma,
            dma((mps,)), dma((mps,)), dma((mps,)), dma((mps,)),
        ],
        compiler_params=pltpu.CompilerParams(
            collective_id=0, has_side_effects=True,
            vmem_limit_bytes=60 << 20,
        ),
    )(
        enc_query[0], enc_keys[0], enc_values[0], enc_lengths, cross_keys[0], cross_values[0],
        cross_query[:, 0, :], dec_query[:, 0, :], dec_keys[:, 0, :], dec_values[:, 0, :],
        cross_out_weight[0], dec_hidden,
    )
    return enc_out[None], self_out[:, None, :], decoded


def solution(mesh):
    in_specs = (
        P("sect", "seq", "mp"),
        P("sect", "seq", "mp"),
        P("sect", "seq", "mp"),
        P(),
        P("sect", "seq", "mp"),
        P("sect", "seq", "mp"),
        P("seq", "mp", "sect"),
        P("seq", "mp", "sect"),
        P("seq", "mp", "sect"),
        P("seq", "mp", "sect"),
        P("mp", "sect", None),
        P("seq", ("sect", "mp")),
    )
    out_specs = (P("sect", "seq", "mp"), P("seq", "mp", "sect"), P("seq", ("sect", "mp")))
    return jax.shard_map(
        functools.partial(per_device, mesh.shape["seq"], mesh.shape["mp"]),
        mesh=mesh, in_specs=in_specs, out_specs=out_specs, check_vma=False,
    )
```

time: 123 us -> 27 us (0.22)
  waiting for transfers between devices: 61.2 us -> 0 us
  blocking collectives: 30.2 us -> 0 us
  Pallas kernels: 0 us -> 23.2 us
  between operations: 14.3 us -> 0.65 us
  local copies, waits for them, and re-layouts: 8.46 us -> 2.96 us
  other arithmetic: 5.31 us -> 0 us
  matrix products: 2.77 us -> 0 us
    reduce_scatter x1 -> x0, waiting for transfers between devices: 54.6 us -> none  [per_device(): lax.psum_scatter(lax.dot_general(weight, cross_context, (((0,), (1,)), ((...]
    all_gather x6 -> x0, blocking collectives: 30.2 us -> none  [the longest x1 6.54 us: per_device(): lax.all_gather(enc_keys, 'seq', axis=1, tiled=True)]
    pallas_call x0 -> x1, Pallas kernels: none -> 23.2 us  [per_device(): pl.pallas_call(functools.partial(kernel, n, mps), out_shape=(jax.ShapeDty...]
    psum x1 -> x0, waiting for transfers between devices: 6.54 us -> none  [broadcast(): return lax.psum(jnp.where(mine, array, jnp.zeros_like(array)), axis)]
    dot_general x7 -> x0, matrix products: 2.77 us -> none  [the longest x1 1.09 us: per_device(): lax.dot_general(weight, cross_context, (((0,), (1,)), ((), ())), preferre...]
    select_n x1 -> x0, other arithmetic: 1.77 us -> none  [broadcast(): return lax.psum(jnp.where(mine, array, jnp.zeros_like(array)), axis)]
    unnamed x22 -> x7, local copies, waits for them, and re-layouts: 4.64 us -> 2.96 us
    dynamic_slice x2 -> x0, local copies, waits for them, and re-layouts: 1.53 us -> none  [the longest x1 0.77 us: per_device(): cross_value_rows = lax.dynamic_slice_in_dim(root_pair[1], offset, narrow, 2)]
  transfers between devices with their start and end apart: 2 -> 0, of which waited for: 2 -> 0; matrix products, arithmetic and copies ran while one was open for 5% -> 0% of each run, Pallas kernels for 0% -> 0%
where the time goes in v1:
time: 27 us; the launch traced here: 26.8 us
  Pallas kernels  23.2 us (86%)
  local copies, waits for them, and re-layouts  2.96 us (11%)
  between operations  0.65 us (2%)
    pallas_call x1, Pallas kernels, per_device(): pl.pallas_call(functools.partial(kernel, n, mps), out_shape=(jax.ShapeDty...  23.2 us
    unnamed x7, local copies, waits for them, and re-layouts  2.96 us

profile of v1, /device:TPU:0, one launch (start us, length us, event | category | flops | bytes accessed | tf_op | source)
XLA Modules:
  0.0 26.8 jit_solution(13857912311780001495)
XLA Ops:
  0.6 23.2 %shard_map.139 = (bf16[128,512]{1,0:T(8,128)(2,1)}, bf16[64,128]{1,0:T(8,128)(2,1)}, bf16[64,256]{1,0:T(8,128)(2,1)}) custom-call(bf16[128,512]{1,0:T(8,128)(2,1)} %bitcast.14, bf16[128,512]{1,0:T(8,128)(2,1)} %bitcast.15, bf16[128,512]{1,0:T(8,128)(2,1)} %bitcast.16, s32[4]{0:T(128)} %lengths.1, bf16[128,512]{1,0:T(8,128)(2,1)} %bitcast.17, ...), custom_call_target="tpu_custom_call" | custom-call | tf_op jit(solution)/shard_map/pallas_call | solution.py:314
  23.8 0.0 copy-start.1
  23.8 1.6 %copy.18 = bf16[1,128,512]{2,1,0:T(8,128)(2,1)} copy(bf16[1,128,512]{2,1,0:T(8,128)(2,1)} %bitcast.13) | data formatting | bytes 262144
  25.4 0.0 copy-done.1
  25.4 0.0 copy-start
  25.4 0.6 %copy.19 = bf16[64,1,128]{2,0,1:T(8,128)(2,1)} copy(bf16[64,1,128]{2,0,1:T(8,128)(2,1)S(1)} %bitcast.23) | data formatting | bytes 32768
  26.0 0.2 copy-done
  26.2 0.6 %copy.20 = bf16[64,256]{1,0:T(8,128)(2,1)} copy(bf16[64,256]{1,0:T(8,128)(2,1)S(1)} %copy-done) | data formatting | bytes 65536
Async XLA Ops:
  23.8 1.6 %copy-start.1 = (bf16[64,128]{1,0:T(8,128)(2,1)S(1)}, bf16[64,128]{1,0:T(8,128)(2,1)}, u32[]{:S(2)}) copy-start(bf16[64,128]{1,0:T(8,128)(2,1)} %get-tuple-element.7) | copy-start | bytes 49156
  25.4 0.8 %copy-start = (bf16[64,256]{1,0:T(8,128)(2,1)S(1)}, bf16[64,256]{1,0:T(8,128)(2,1)}, u32[]{:S(2)}) copy-start(bf16[64,256]{1,0:T(8,128)(2,1)} %get-tuple-element.14) | copy-start | bytes 98308

commit v2 on v1

--- a/solution.py
+++ b/solution.py
@@ -157,27 +157,27 @@
     def _():
         all_cross(start_cross)
 
-    def seq_copies(step):
+    def seq_copies(group, step):
         device = {"seq": peer(step)}
-        dec = [
-            remote(source, target.at[seq], dec_send.at[which, step], dec_recv.at[which, seq], device)
-            for which, source, target in ((0, dk, dkb), (1, dv, dvb))
-        ]
-        enc = [
+        if group == 0:
+            return [
+                remote(source, target.at[seq], dec_send.at[which, step], dec_recv.at[which, seq], device)
+                for which, source, target in ((0, dk, dkb), (1, dv, dvb))
+            ]
+        return [
             remote(source, target.at[seq], enc_send.at[which, step], enc_recv.at[which, seq], device)
             for which, source, target in ((0, ek, ekb), (1, ev, evb))
         ]
-        return dec + enc
-
-    def start_seq(step):
-        for copy in seq_copies(step):
+
+    def start_seq(group, step):
+        for copy in seq_copies(group, step):
             copy.start()
 
     def end_seq(step):
-        for copy in seq_copies(step):
+        for copy in seq_copies(0, step) + seq_copies(1, step):
             copy.wait_send()
 
-    each(1, n, start_seq)
+    each(1, n, functools.partial(start_seq, 0))
     w_copies = [
         remote(weight.at[:, columns(half, 1 - core)], w_v.at[half, pl.ds(depth, depth)],
                w_send.at[half], w_recv.at[half], {"sect": near})
@@ -218,6 +218,7 @@
         landed(xvb.at[source], x_recv.at[1, source])
 
     each(0, n, cross_landed)
+    each(1, n, functools.partial(start_seq, 1))
     length = n * enc_rows
     position = lax.broadcasted_iota(jnp.int32, (1, length), 1)
     bias = jnp.where(position < lengths[0], 0.0, LOW)
@@ -268,10 +269,6 @@
     for step in order:
         own[step] = project(level, step)
 
-    each(1, n, lambda step: enc_chunk(peer(step), False))
-    for pair in range(pairs):
-        enc_out[:, pair * PAIR:(pair + 1) * PAIR] = merge_heads(acc[pair])
-
     z_copies = {}
     for step in range(1, mps):
         y_copies[step].wait_recv()
@@ -281,6 +278,10 @@
             {"mp": lax.rem(mp + step, mps)},
         )
         z_copies[step].start()
+    each(1, n, lambda step: enc_chunk(peer(step), False))
+    for pair in range(pairs):
+        enc_out[:, pair * PAIR:(pair + 1) * PAIR] = merge_heads(acc[pair])
+
     loads[3].wait()
     y_copies[0].wait_recv()
     total = own[0] + y_in[0].astype(F32)
@@ -296,6 +297,18 @@
     each(1, n, end_seq)
     for copy in w_copies + [ctx_copy] + list(y_copies.values()) + list(z_copies.values()):
         copy.wait_send()
+
+
+def store(*refs):
+    sources, targets, sems = refs[:3], refs[3:6], refs[6]
+    copies = [
+        pltpu.make_async_copy(source, target, sems.at[which])
+        for which, (source, target) in enumerate(zip(sources, targets))
+    ]
+    for copy in copies:
+        copy.start()
+    for copy in copies:
+        copy.wait()
 
 
 def per_device(
@@ -309,18 +322,15 @@
     span = model // SECTIONS
     pairs = enc_width // PAIR
     vmem, dma = pltpu.VMEM, pltpu.SemaphoreType.DMA
-    any_space = pl.BlockSpec(memory_space=pl.ANY)
+    in_hbm = pl.BlockSpec(memory_space=pltpu.HBM)
     in_vmem = pl.BlockSpec(memory_space=pltpu.VMEM)
-    enc_out, self_out, decoded = pl.pallas_call(
+    shapes = ((enc_rows, enc_width), (dec_rows, narrow), (dec_rows, block))
+    results = pl.pallas_call(
         functools.partial(kernel, n, mps),
-        out_shape=(
-            jax.ShapeDtypeStruct((enc_rows, enc_width), BF16),
-            jax.ShapeDtypeStruct((dec_rows, narrow), BF16),
-            jax.ShapeDtypeStruct((dec_rows, block), BF16),
-        ),
-        in_specs=[any_space] * 3
+        out_shape=tuple(vmem(shape, BF16) for shape in shapes),
+        in_specs=[in_hbm] * 3
         + [pl.BlockSpec(memory_space=pltpu.SMEM)]
-        + [any_space] * 8,
+        + [in_hbm] * 8,
         out_specs=(in_vmem,) * 3,
         scratch_shapes=[
             vmem((enc_rows, enc_width), BF16),
@@ -360,6 +370,13 @@
         cross_query[:, 0, :], dec_query[:, 0, :], dec_keys[:, 0, :], dec_values[:, 0, :],
         cross_out_weight[0], dec_hidden,
     )
+    enc_out, self_out, decoded = pl.pallas_call(
+        store,
+        out_shape=tuple(jax.ShapeDtypeStruct(shape, BF16) for shape in shapes),
+        in_specs=[in_vmem] * 3,
+        out_specs=(in_hbm,) * 3,
+        scratch_shapes=[dma((3,))],
+    )(*results)
     return enc_out[None], self_out[:, None, :], decoded
 
 

time: 27 us -> 25 us (0.926)
  local copies, waits for them, and re-layouts: 2.96 us -> 1.85 us
  Pallas kernels: 23.2 us -> 22.3 us
    unnamed x7 -> x6, local copies, waits for them, and re-layouts: 2.96 us -> 1.85 us
    pallas_call x1 -> x2, Pallas kernels: 23.2 us -> 22.3 us  [the longest x1 20.7 us: per_device(): pl.pallas_call(functools.partial(kernel, n, mps), out_shape=tuple((vmem(s...]
where the time goes in v2:
time: 25 us; the launch traced here: 24.8 us
  Pallas kernels  22.3 us (89%)
  local copies, waits for them, and re-layouts  1.85 us (7%)
  between operations  0.65 us (3%)
    pallas_call x1, Pallas kernels, per_device(): pl.pallas_call(functools.partial(kernel, n, mps), out_shape=tuple((vmem(s...  20.7 us
    unnamed x6, local copies, waits for them, and re-layouts  1.85 us
    pallas_call x1, Pallas kernels, per_device(): pl.pallas_call(store, out_shape=tuple((jax.ShapeDtypeStruct(shape, BF16)...  1.61 us

profile of v2, /device:TPU:0, one launch (start us, length us, event | category | flops | bytes accessed | tf_op | source)
XLA Modules:
  0.0 24.8 jit_solution(14278017287625690645)
XLA Ops:
  0.6 20.7 %shard_map.139 = (bf16[128,512]{1,0:T(8,128)(2,1)S(1)}, bf16[64,128]{1,0:T(8,128)(2,1)S(1)}, bf16[64,256]{1,0:T(8,128)(2,1)S(1)}) custom-call(bf16[128,512]{1,0:T(8,128)(2,1)} %bitcast.13, bf16[128,512]{1,0:T(8,128)(2,1)} %bitcast.14, bf16[128,512]{1,0:T(8,128)(2,1)} %bitcast.15, s32[4]{0:T(128)} %lengths.1, bf16[128,512]{1,0:T(8,128)(2,1)} %bitcast.16, ...), custom_call_target="tpu_custom_call" | custom-call | tf_op jit(solution)/shard_map/pallas_call | solution.py:328
  21.4 0.0 copy-start
  21.4 0.6 %copy-done = bf16[128,512]{1,0:T(8,128)(2,1)} copy-done((bf16[128,512]{1,0:T(8,128)(2,1)}, bf16[128,512]{1,0:T(8,128)(2,1)S(1)}, u32[]{:S(2)}) %copy-start) | copy-done | bytes 131096
  22.0 0.0 copy-start.1
  22.0 0.6 %copy-done.1 = bf16[64,256]{1,0:T(8,128)(2,1)} copy-done((bf16[64,256]{1,0:T(8,128)(2,1)}, bf16[64,256]{1,0:T(8,128)(2,1)S(1)}, u32[]{:S(2)}) %copy-start.1) | copy-done | bytes 32792
  22.6 0.0 copy-start.2
  22.6 0.6 %copy-done.2 = bf16[64,128]{1,0:T(8,128)(2,1)} copy-done((bf16[64,128]{1,0:T(8,128)(2,1)}, bf16[64,128]{1,0:T(8,128)(2,1)S(1)}, u32[]{:S(2)}) %copy-start.2) | copy-done | bytes 16408
  23.2 1.6 %shard_map.140 = (bf16[128,512]{1,0:T(8,128)(2,1)}, bf16[64,128]{1,0:T(8,128)(2,1)}, bf16[64,256]{1,0:T(8,128)(2,1)}) custom-call(bf16[128,512]{1,0:T(8,128)(2,1)} %copy-done, bf16[64,128]{1,0:T(8,128)(2,1)} %copy-done.2, bf16[64,256]{1,0:T(8,128)(2,1)} %copy-done.1), custom_call_target="tpu_custom_call" | custom-call | tf_op jit(solution)/shard_map/pallas_call | solution.py:373
Async XLA Ops:
  21.4 0.7 %copy-start = (bf16[128,512]{1,0:T(8,128)(2,1)}, bf16[128,512]{1,0:T(8,128)(2,1)S(1)}, u32[]{:S(2)}) copy-start(bf16[128,512]{1,0:T(8,128)(2,1)S(1)} %get-tuple-element.9.refs_0_) | copy-start | bytes 393220
  22.0 0.6 %copy-start.1 = (bf16[64,256]{1,0:T(8,128)(2,1)}, bf16[64,256]{1,0:T(8,128)(2,1)S(1)}, u32[]{:S(2)}) copy-start(bf16[64,256]{1,0:T(8,128)(2,1)S(1)} %get-tuple-element.11.refs_2_) | copy-start | bytes 98308
  22.6 0.6 %copy-start.2 = (bf16[64,128]{1,0:T(8,128)(2,1)}, bf16[64,128]{1,0:T(8,128)(2,1)S(1)}, u32[]{:S(2)}) copy-start(bf16[64,128]{1,0:T(8,128)(2,1)S(1)} %get-tuple-element.10.refs_1_) | copy-start | bytes 49156

commit v3 on v2

--- a/solution.py
+++ b/solution.py
@@ -376,6 +376,7 @@
         in_specs=[in_vmem] * 3,
         out_specs=(in_hbm,) * 3,
         scratch_shapes=[dma((3,))],
+        compiler_params=pltpu.CompilerParams(vmem_limit_bytes=1 << 20),
     )(*results)
     return enc_out[None], self_out[:, None, :], decoded
 

time: 25 us -> 22.2 us (0.89)
  local copies, waits for them, and re-layouts: 1.85 us -> 0 us
  Pallas kernels: 22.3 us -> 21.4 us
    unnamed x6 -> x0, local copies, waits for them, and re-layouts: 1.85 us -> none
    pallas_call x1, Pallas kernels: 1.61 us -> 0.69 us  [per_device(): pl.pallas_call(store, out_shape=tuple((jax.ShapeDtypeStruct(shape, BF16)...]
where the time goes in v3:
time: 22.2 us; the launch traced here: 22.1 us
  Pallas kernels  21.4 us (96%)
  between operations  0.64 us (3%)
    pallas_call x1, Pallas kernels, per_device(): pl.pallas_call(functools.partial(kernel, n, mps), out_shape=tuple((vmem(s...  20.7 us
    pallas_call x1, Pallas kernels, per_device(): pl.pallas_call(store, out_shape=tuple((jax.ShapeDtypeStruct(shape, BF16)...  0.69 us

profile of v3, /device:TPU:0, one launch (start us, length us, event | category | flops | bytes accessed | tf_op | source)
XLA Modules:
  0.0 22.1 jit_solution(15430848789415158094)
XLA Ops:
  0.6 20.7 %shard_map.139 = (bf16[128,512]{1,0:T(8,128)(2,1)S(1)}, bf16[64,128]{1,0:T(8,128)(2,1)S(1)}, bf16[64,256]{1,0:T(8,128)(2,1)S(1)}) custom-call(bf16[128,512]{1,0:T(8,128)(2,1)} %bitcast.13, bf16[128,512]{1,0:T(8,128)(2,1)} %bitcast.14, bf16[128,512]{1,0:T(8,128)(2,1)} %bitcast.15, s32[4]{0:T(128)} %lengths.1, bf16[128,512]{1,0:T(8,128)(2,1)} %bitcast.16, ...), custom_call_target="tpu_custom_call" | custom-call | tf_op jit(solution)/shard_map/pallas_call | solution.py:328
  21.4 0.7 %shard_map.140 = (bf16[128,512]{1,0:T(8,128)(2,1)}, bf16[64,128]{1,0:T(8,128)(2,1)}, bf16[64,256]{1,0:T(8,128)(2,1)}) custom-call(bf16[128,512]{1,0:T(8,128)(2,1)S(1)} %get-tuple-element.9.refs_0_, bf16[64,128]{1,0:T(8,128)(2,1)S(1)} %get-tuple-element.10.refs_1_, bf16[64,256]{1,0:T(8,128)(2,1)S(1)} %get-tuple-element.11.refs_2_), custom_call_target="tpu_custom_call" | custom-call | tf_op jit(solution)/shard_map/pallas_call | solution.py:373

commit v4 on v3

--- a/solution.py
+++ b/solution.py
@@ -229,6 +229,29 @@
     ctx_copy = remote(ctx, ctx_in, ctx_send, ctx_recv, {"sect": near})
     ctx_copy.start()
 
+    for load in w_loads:
+        load.wait()
+    for copy in w_copies:
+        copy.wait_recv()
+    ctx_copy.wait_recv()
+    both = jnp.concatenate([ctx[...], ctx_in[...]], axis=1)
+    order = list(range(1, mps)) + [0]
+
+    def project(half, step):
+        owner = lax.rem(mp + step, mps)
+        lanes = pl.ds(pl.multiple_of(owner * block, block), block)
+        return jnp.dot(both, w_v[half, :, lanes], preferred_element_type=F32)
+
+    y_copies = {}
+    for step in order:
+        y_out[step] = project(1 - level, step).astype(BF16)
+        y_copies[step] = remote(
+            y_out.at[step], y_in.at[step], y_send.at[step], y_recv.at[step], {"sect": far}
+        )
+        y_copies[step].start()
+    for step in order:
+        own[step] = project(level, step)
+
     loads[2].wait()
 
     def dec_landed(source):
@@ -245,29 +268,6 @@
         stack_heads(dq_v[...]), dkb[...].reshape(length, PAIR), dvb[...].reshape(length, PAIR), bias
     )
     self_out[...] = merge_heads(summed)
-
-    for load in w_loads:
-        load.wait()
-    for copy in w_copies:
-        copy.wait_recv()
-    ctx_copy.wait_recv()
-    both = jnp.concatenate([ctx[...], ctx_in[...]], axis=1)
-    order = list(range(1, mps)) + [0]
-
-    def project(half, step):
-        owner = lax.rem(mp + step, mps)
-        lanes = pl.ds(pl.multiple_of(owner * block, block), block)
-        return jnp.dot(both, w_v[half, :, lanes], preferred_element_type=F32)
-
-    y_copies = {}
-    for step in order:
-        y_out[step] = project(1 - level, step).astype(BF16)
-        y_copies[step] = remote(
-            y_out.at[step], y_in.at[step], y_send.at[step], y_recv.at[step], {"sect": far}
-        )
-        y_copies[step].start()
-    for step in order:
-        own[step] = project(level, step)
 
     z_copies = {}
     for step in range(1, mps):

time: 22.2 us -> 22.2 us (level)
  no operation moved by 1% of the time
where the time goes in v4:
time: 22.2 us; the launch traced here: 22.1 us
  Pallas kernels  21.4 us (96%)
  between operations  0.64 us (3%)
    pallas_call x1, Pallas kernels, per_device(): pl.pallas_call(functools.partial(kernel, n, mps), out_shape=tuple((vmem(s...  20.7 us
    pallas_call x1, Pallas kernels, per_device(): pl.pallas_call(store, out_shape=tuple((jax.ShapeDtypeStruct(shape, BF16)...  0.69 us

profile of v4, /device:TPU:0, one launch (start us, length us, event | category | flops | bytes accessed | tf_op | source)
XLA Modules:
  0.0 22.1 jit_solution(3944816237197296981)
XLA Ops:
  0.6 20.7 %shard_map.139 = (bf16[128,512]{1,0:T(8,128)(2,1)S(1)}, bf16[64,128]{1,0:T(8,128)(2,1)S(1)}, bf16[64,256]{1,0:T(8,128)(2,1)S(1)}) custom-call(bf16[128,512]{1,0:T(8,128)(2,1)} %bitcast.13, bf16[128,512]{1,0:T(8,128)(2,1)} %bitcast.14, bf16[128,512]{1,0:T(8,128)(2,1)} %bitcast.15, s32[4]{0:T(128)} %lengths.1, bf16[128,512]{1,0:T(8,128)(2,1)} %bitcast.16, ...), custom_call_target="tpu_custom_call" | custom-call | tf_op jit(solution)/shard_map/pallas_call | solution.py:328
  21.4 0.7 %shard_map.140 = (bf16[128,512]{1,0:T(8,128)(2,1)}, bf16[64,128]{1,0:T(8,128)(2,1)}, bf16[64,256]{1,0:T(8,128)(2,1)}) custom-call(bf16[128,512]{1,0:T(8,128)(2,1)S(1)} %get-tuple-element.9.refs_0_, bf16[64,128]{1,0:T(8,128)(2,1)S(1)} %get-tuple-element.10.refs_1_, bf16[64,256]{1,0:T(8,128)(2,1)S(1)} %get-tuple-element.11.refs_2_), custom_call_target="tpu_custom_call" | custom-call | tf_op jit(solution)/shard_map/pallas_call | solution.py:373

commit v5 on v3

--- a/solution.py
+++ b/solution.py
@@ -186,6 +186,10 @@
     for copy in w_copies:
         copy.start()
 
+    @pl.when(level == 1)
+    def _():
+        each(1, n, functools.partial(start_seq, 1))
+
     enc_limit = lengths[sect]
     pairs = enc_width // PAIR
 
@@ -218,7 +222,11 @@
         landed(xvb.at[source], x_recv.at[1, source])
 
     each(0, n, cross_landed)
-    each(1, n, functools.partial(start_seq, 1))
+
+    @pl.when(level == 0)
+    def _():
+        each(1, n, functools.partial(start_seq, 1))
+
     length = n * enc_rows
     position = lax.broadcasted_iota(jnp.int32, (1, length), 1)
     bias = jnp.where(position < lengths[0], 0.0, LOW)

time: 22.2 us -> 22.6 us (1.018)
  Pallas kernels: 21.4 us -> 21.8 us
    pallas_call x1, Pallas kernels: 20.7 us -> 21.1 us  [per_device(): pl.pallas_call(functools.partial(kernel, n, mps), out_shape=tuple((vmem(s...]
where the time goes in v5:
time: 22.6 us; the launch traced here: 22.4 us
  Pallas kernels  21.8 us (96%)
  between operations  0.64 us (3%)
    pallas_call x1, Pallas kernels, per_device(): pl.pallas_call(functools.partial(kernel, n, mps), out_shape=tuple((vmem(s...  21.1 us
    pallas_call x1, Pallas kernels, per_device(): pl.pallas_call(store, out_shape=tuple((jax.ShapeDtypeStruct(shape, BF16)...  0.69 us

profile of v5, /device:TPU:0, one launch (start us, length us, event | category | flops | bytes accessed | tf_op | source)
XLA Modules:
  0.0 22.4 jit_solution(16915389498448487250)
XLA Ops:
  0.6 21.1 %shard_map.139 = (bf16[128,512]{1,0:T(8,128)(2,1)S(1)}, bf16[64,128]{1,0:T(8,128)(2,1)S(1)}, bf16[64,256]{1,0:T(8,128)(2,1)S(1)}) custom-call(bf16[128,512]{1,0:T(8,128)(2,1)} %bitcast.13, bf16[128,512]{1,0:T(8,128)(2,1)} %bitcast.14, bf16[128,512]{1,0:T(8,128)(2,1)} %bitcast.15, s32[4]{0:T(128)} %lengths.1, bf16[128,512]{1,0:T(8,128)(2,1)} %bitcast.16, ...), custom_call_target="tpu_custom_call" | custom-call | tf_op jit(solution)/shard_map/pallas_call | solution.py:336
  21.7 0.7 %shard_map.140 = (bf16[128,512]{1,0:T(8,128)(2,1)}, bf16[64,128]{1,0:T(8,128)(2,1)}, bf16[64,256]{1,0:T(8,128)(2,1)}) custom-call(bf16[128,512]{1,0:T(8,128)(2,1)S(1)} %get-tuple-element.9.refs_0_, bf16[64,128]{1,0:T(8,128)(2,1)S(1)} %get-tuple-element.10.refs_1_, bf16[64,256]{1,0:T(8,128)(2,1)S(1)} %get-tuple-element.11.refs_2_), custom_call_target="tpu_custom_call" | custom-call | tf_op jit(solution)/shard_map/pallas_call | solution.py:381
